TPU v7x, 256 devices: a whole 4x4x8 slice. The times are simulated.
256 devices in a mesh: tm: 8 (over y, core), tile: 32 (over x, z).
Axes of the slice: x: 4, y: 4, z: 8, core: 2. Of those that a mesh axis runs over, the one named last changes fastest.
Arguments:
- frames: bfloat16 [8, 4, 4096, 1024], P('tm', None, 'tile'), may hold values from -6 to 6
- peaks: int32 [8, 4, 2048], P('tm', None, 'tile'), may hold values from -10 to 10
- calib: float32 [12, 2048], P(None, 'tile'), may hold values from -1.25 to 1.25
- counts: int32 [32], P('tile'), may hold values from 16 to 64, as said below
- owner: int32 [2048, 1], P('tile'), may hold values from 0 to 31; in each aligned block of 64 rows (0 to 63, 64 to 127, ...) at most 4 rows name the same one
- cell: int32 [2048], P('tile'), may hold values from 0 to 2047
- spread: float32 [8, 2048], P(None, 'tile'), may hold values from 0.5 to 2
- start: int32 [1], replicated, may hold values from 0 to 4087
Outputs:
- spectrum: float32 [16, 6, 65536], P('tm', None, 'tile')
Inputs may be any that keep to these rules, and one draw needn't show every extreme that they name: `counts`: the valid windows of a tile are its last ones in row-major order; some tile has all 64 valid. Among the 64 windows of one tile at most 4 name the same owner.
All inputs are finite; a program needn't handle non-finite values.
Results may differ from a plain program's by a relative error of at most 0.0003.
Values may be sent and summed in bfloat16 or wider, within the bound.
A program may use at most 64 MiB of HBM per device.

v0:
```python
import functools
import math

import jax
import jax.numpy as jnp
import ml_dtypes
import numpy as np
from jax import lax
from jax.experimental import pallas as pl
from jax.experimental.pallas import tpu as pltpu
from jax.sharding import PartitionSpec as P

WIN = 64
HALF = 32
FREQS = 16
NFFT = 4096
AZ = 512
SPREAD = 8
CAP = 4
GROUP = 256
WINS = 64
SHARPNESS = 20.0
MESH = pl.DeviceIdType.MESH
BF = jnp.bfloat16
F32 = jnp.float32
N_TM = 8
N_TILE = 32


def _pair(table):
    hi = table.astype(ml_dtypes.bfloat16)
    lo = (table - hi.astype(np.float64)).astype(ml_dtypes.bfloat16)
    return hi, lo


def _real_dft():
    n = np.arange(WIN)
    k = np.arange(HALF)[:, None]
    cos = np.round(np.cos(2.0 * np.pi * ((k * n) % WIN) / WIN), 14)
    sin = np.round(np.sin(2.0 * np.pi * ((k * n) % WIN) / WIN), 14)
    sin[0] = 1.0 - 2.0 * (n % 2)
    return cos, sin


def _tables():
    cos, sin = _real_dft()
    weight = np.where(np.arange(HALF) == 0, 1.0, 2.0)[:, None]
    eye = np.eye(4)
    fx = np.concatenate([np.kron(eye, cos.T), np.kron(eye, sin.T)], axis=1)
    ix = np.concatenate([np.kron(eye, weight * cos), np.kron(eye, weight * sin)], axis=0)
    fy = np.zeros((2, 3, HALF, 128))
    for r in range(3):
        fy[0, r, :, r * HALF : r * HALF + WIN] = cos
        fy[1, r, :, r * HALF : r * HALF + WIN] = sin
    fy = fy.reshape(192, 128)
    fyb = np.concatenate([cos, sin], axis=0)
    iy = np.concatenate([weight * cos, weight * sin], axis=0).T
    fx_hi, fx_lo = _pair(fx)
    ix_hi, ix_lo = _pair(ix)
    fy_hi, fy_lo = _pair(fy)
    fyb_hi, fyb_lo = _pair(fyb)
    iy_hi, iy_lo = _pair(iy)
    cat = np.concatenate
    return (
        np.stack([fx_hi, fx_lo]),
        np.stack([ix_hi, ix_lo]),
        cat([fy_hi, fy_hi], axis=1),
        fy_lo,
        cat([fyb_hi, fyb_hi, fyb_lo], axis=1),
        cat([iy_hi, iy_hi, iy_lo], axis=1),
    )


def dot(lhs, rhs):
    return jnp.dot(lhs, rhs, preferred_element_type=F32)


def dot_t(lhs, rhs):
    return lax.dot_general(lhs, rhs, (((1,), (1,)), ((), ())), preferred_element_type=F32)


def split2(x):
    hi = x.astype(BF)
    return hi, (x - hi.astype(F32)).astype(BF)


def split3(x):
    hi = x.astype(BF)
    rest = x - hi.astype(F32)
    mid = rest.astype(BF)
    return hi, mid, (rest - mid.astype(F32)).astype(BF)


def iota(shape, dim):
    return lax.broadcasted_iota(jnp.int32, shape, dim)


def cross(first, second, y0, x0):
    a, b, c, d = first
    a2, b2, c2, d2 = second
    aa, bb, cc, dd = a * a2, b * b2, c * c2, d * d2
    ac, bd = a * c2 - c * a2, b * d2 - d * b2
    ab, cd = a * b2 - b * a2, c * d2 - d * c2
    ad, bc = a * d2 + d * a2, b * c2 + c * b2
    low, high = jnp.where(x0, aa, aa + cc), jnp.where(x0, bb, bb + dd)
    low_s, high_s = jnp.where(x0, cc, ac), jnp.where(x0, dd, bd)
    p_cc = jnp.where(y0, low, low + high)
    p_cs = jnp.where(y0, low_s, jnp.where(x0, cc + dd, ac + bd))
    p_sc = jnp.where(y0, high, jnp.where(x0, ab, ab + cd))
    p_ss = jnp.where(y0, high_s, jnp.where(x0, cd, ad - bc))
    return p_cc, p_cs, p_sc, p_ss


def parts(t, half):
    return t[:half, :128], t[half:, :128], t[:half, 128:], t[half:, 128:]


def inverse_x(spectra, ix):
    rows = []
    for p_cc, p_cs, p_sc, p_ss in spectra:
        rows.append(jnp.concatenate([p_cc, p_cs], axis=1))
        rows.append(jnp.concatenate([p_sc, p_ss], axis=1))
    hi, lo = split2(jnp.concatenate(rows, axis=0))
    return dot(hi, ix[0]) + dot(lo, ix[0]) + dot(hi, ix[1])


def energy_rows(four, weight, bands):
    a, b, c, d = four
    e = (a * a + b * b) + (c * c + d * d)
    return [
        jnp.sum(e[r * HALF : (r + 1) * HALF] * weight, axis=0, keepdims=True) for r in range(bands)
    ]


def inverse_norm(rows, spread_lanes):
    have = len(rows)
    padded = rows + [jnp.zeros((16 - have, 128), F32)] * (have < 16)
    hi, mid, lo = split3(jnp.concatenate(padded, axis=0))
    wide = dot(jnp.concatenate([hi, mid, lo], axis=0), spread_lanes)
    total = wide[0:16] + wide[16:32] + wide[32:48]
    return lax.rsqrt(total * (1.0 / 4096.0**2) + 1e-5)


def wrapped(lag, peak):
    off = lag - peak
    return jnp.where(off >= 32.0, off - 64.0, off)


def correlate_and_send(
    frames, fx, ix, fy2, fy_lo, fyb, iy, peaks, calib, counts, owner, cell, spread, start,
    got_ref,
    image, halo, edge_hi, edge_lo, peak_lanes, stats, vecs, outbox, inbox,
    load_sem, halo_send, halo_recv, vec_send, vec_recv, box_send, box_recv,
):
    tm, tile = lax.axis_index("tm"), lax.axis_index("tile")
    above, below = lax.rem(tile + N_TILE - 1, N_TILE), lax.rem(tile + 1, N_TILE)

    load = pltpu.make_async_copy(frames.at[0], image, load_sem)
    load.start()

    barrier = pltpu.get_barrier_semaphore()

    def greet_tm(i, _):
        pl.semaphore_signal(
            barrier, 1, device_id=(lax.rem(tm + i, N_TM), tile), device_id_type=MESH
        )
        return _

    def greet_tile(i, _):
        pl.semaphore_signal(
            barrier, 1, device_id=(tm, lax.rem(tile + i, N_TILE)), device_id_type=MESH
        )
        return _

    lax.fori_loop(1, N_TM, greet_tm, 0)
    lax.fori_loop(1, N_TILE, greet_tile, 0)

    stats[...] = jnp.zeros_like(stats)
    peak = peaks[0].astype(F32)
    band_of = iota((4, WINS), 1) // 16
    picks = jnp.concatenate(
        [
            jnp.where(iota((4, WINS), 0) == band_of, jnp.broadcast_to(peak[j : j + 1], (4, WINS)), 0.0)
            for j in range(4)
        ],
        axis=0,
    ).astype(BF)
    to_lanes = (iota((WINS, 1024), 0) % 16 == iota((WINS, 1024), 1) // WIN).astype(F32).astype(BF)
    peak_lanes[...] = dot(picks, to_lanes)

    pl.semaphore_wait(barrier, N_TM + N_TILE - 2)
    halo_copy = pltpu.make_async_remote_copy(
        src_ref=frames.at[0, :, pl.ds(0, HALF), :],
        dst_ref=halo,
        send_sem=halo_send,
        recv_sem=halo_recv,
        device_id=(tm, above),
        device_id_type=MESH,
    )
    halo_copy.start()
    load.wait()

    weight = jnp.where(iota((HALF, 128), 0) == 0, 1.0, 2.0) * jnp.where(
        iota((HALF, 128), 1) % HALF == 0, 1.0, 2.0
    )
    spread_lanes = (iota((128, GROUP), 0) // HALF == iota((128, GROUP), 1) // WIN).astype(F32)
    spread_lanes = spread_lanes.astype(BF)
    row_lag = iota((WIN, GROUP), 0).astype(F32)
    col_lag = (iota((1, GROUP), 1) % WIN).astype(F32)
    gain = SHARPNESS * math.log2(math.e) / 4096.0**2

    def slots(bands):
        shape = (bands * HALF, 128)
        y0, x0 = iota(shape, 0) % HALF == 0, iota(shape, 1) % HALF == 0
        return y0, x0, y0 & x0

    def correlate(t, bands, first_band, lanes, span):
        half = bands * HALF
        y0, x0, dc = slots(bands)
        four = []
        for one in t:
            a, b, c, d = parts(one, half)
            four.append((jnp.where(dc, 0.0, a), b, c, d))
        energies = [row for one in four for row in energy_rows(one, weight, bands)]
        scale = inverse_norm(energies, spread_lanes)
        spectra = [cross(four[2 * cam], four[2 * cam + 1], y0, x0) for cam in range(2)]
        z_hi, z_lo = split2(inverse_x(spectra, ix))
        for cam in range(2):
            for r in range(bands):
                at = [(cam * 2 + part) * half + r * HALF for part in range(2)]
                hi = [z_hi[i : i + HALF] for i in at]
                lo = [z_lo[i : i + HALF] for i in at]
                corr = dot(iy[...], jnp.concatenate(hi + lo + hi, axis=0))
                i, j = (2 * cam) * bands + r, (2 * cam + 1) * bands + r
                p = jnp.exp2(corr * (scale[i : i + 1] * scale[j : j + 1] * gain))
                band = first_band + r
                i, j = 8 * cam + band, 8 * cam + 4 + band
                rows_at = peak_lanes[i : i + 1, pl.ds(lanes, span)]
                cols_at = peak_lanes[j : j + 1, pl.ds(lanes, span)]
                total = jnp.sum(p, axis=0, keepdims=True)
                by_row = jnp.sum(p * wrapped(row_lag, rows_at), axis=0, keepdims=True)
                by_col = total * wrapped(col_lag, cols_at)
                for k, value in enumerate((total, by_row, by_col)):
                    i = band * 8 + k * 2 + cam
                    stats[i : i + 1, pl.ds(lanes, span)] = value

    def own_bands(g, carry):
        lanes = pl.multiple_of(g * GROUP, GROUP)
        pixels = image[:, :, pl.ds(lanes, GROUP)].reshape(4 * 128, GROUP)
        x_hi, x_lo = split2(dot(pixels, fx[0]) + dot(pixels, fx[1]))
        t = []
        for f in range(4):
            hi, lo = x_hi[f * 128 : (f + 1) * 128], x_lo[f * 128 : (f + 1) * 128]
            edge_hi[f, :, pl.ds(lanes, GROUP)] = hi[96:]
            edge_lo[f, :, pl.ds(lanes, GROUP)] = lo[96:]
            t.append(dot(fy2[...], jnp.concatenate([hi, lo], axis=0)) + dot(fy_lo[...], hi))
        correlate(t, 3, 0, lanes, GROUP)
        return carry

    lax.fori_loop(0, 4, own_bands, 0)

    halo_copy.wait()

    def last_band(g, carry):
        lanes = pl.multiple_of(g * GROUP, GROUP)
        pixels = halo[:, :, pl.ds(lanes, GROUP)].reshape(4 * HALF, GROUP)
        x = dot(pixels, fx[0]) + dot(pixels, fx[1])
        x_hi, x_lo = split2(jnp.where(tile == N_TILE - 1, 0.0, x))
        t = []
        for f in range(4):
            hi = [edge_hi[f, :, pl.ds(lanes, GROUP)], x_hi[f * HALF : (f + 1) * HALF]]
            lo = [edge_lo[f, :, pl.ds(lanes, GROUP)], x_lo[f * HALF : (f + 1) * HALF]]
            t.append(dot(fyb[...], jnp.concatenate(hi + lo + hi, axis=0)))
        correlate(t, 1, 3, lanes, GROUP)
        return carry

    lax.fori_loop(0, 4, last_band, 0)

    lane = iota((8, 128), 1)
    window = lane % WINS
    to_window = (iota((1024, 128), 0) // WIN == iota((1024, 128), 1) % 16).astype(F32).astype(BF)
    hi, mid, lo = split3(stats[...])
    y = dot(jnp.concatenate([hi, mid, lo], axis=0), to_window)
    y = y[0:32] + y[32:64] + y[64:96]
    y = sum(jnp.where(window // 16 == r, y[8 * r : 8 * r + 8], 0.0) for r in range(4))
    peak2 = jnp.concatenate([peak, peak], axis=1)
    inverse = 1.0 / y[0:2]
    disp = []
    for cam in range(2):
        for part in range(2):
            j, i = 2 * cam + part, 2 + 2 * part + cam
            disp.append(peak2[j : j + 1] + y[i : i + 1] * inverse[cam : cam + 1])
    live = (window >= WINS - counts[0]).astype(F32)
    calib2 = jnp.concatenate([calib[...], calib[...]], axis=1)
    vec = []
    for i in range(3):
        vec.append(sum(calib2[4 * i + j : 4 * i + j + 1] * disp[j] for j in range(4)))
    six = jnp.concatenate(vec + vec + [jnp.zeros((2, 128), F32)], axis=0) * live
    vecs[pl.ds(tm, 1)] = six[None]

    def vec_copy(i):
        peer = lax.rem(tm + i, N_TM)
        return pltpu.make_async_remote_copy(
            src_ref=vecs.at[tm],
            dst_ref=vecs.at[tm],
            send_sem=vec_send,
            recv_sem=vec_recv,
            device_id=(peer, tile),
            device_id_type=MESH,
        )

    for i in range(1, N_TM):
        vec_copy(i).start()

    owners = jnp.concatenate([owner[...], owner[...]], axis=0)
    named = (owners == iota((128, 128), 1)).astype(F32)
    hits = named.T[0:N_TILE]
    before = ((iota((128, 128), 0) < iota((128, 128), 1) % WINS) & (iota((128, 128), 0) < WINS))
    earlier = dot(hits.astype(BF), before.astype(F32).astype(BF))
    rank = jnp.sum(hits * earlier, axis=0, keepdims=True)
    half = (iota((1, 128), 1) // WINS).astype(F32)
    place = jnp.concatenate(
        [jnp.where(rank == half, hits, 0.0), jnp.where(rank == half + 2.0, hits, 0.0)], axis=1
    ).astype(BF)
    cells = cell[...].astype(F32)
    cells = jnp.broadcast_to(jnp.concatenate([cells, cells], axis=1), (8, 128))
    spread2 = jnp.concatenate([spread[...], spread[...]], axis=1) * live
    part = iota((8, 128), 0)
    turn = jnp.where(part >= 3, 4, 0)
    coefs = []
    for k in range(2):
        freq = tm * 2 + k
        for s in range(N_TM):
            n = (freq * (start[0] + s) + turn) & 15
            value = jnp.zeros((8, 128), F32)
            for step in range(16):
                value = jnp.where(n == step, math.cos(2.0 * math.pi * step / 16), value)
            coefs.append(value)

    pltpu.make_async_copy(vecs.at[pl.ds(0, 7)], vecs.at[pl.ds(0, 7)], vec_send).wait()
    pltpu.make_async_copy(vecs.at[pl.ds(0, 7)], vecs.at[pl.ds(0, 7)], vec_recv).wait()
    fourier = [
        sum(coefs[k * N_TM + s] * vecs[s] for s in range(N_TM)) for k in range(2)
    ]
    fourier[0] = jnp.where(part == 6, 1.0, fourier[0])
    payload = jnp.concatenate(fourier + [spread2, cells], axis=0)
    first = iota((32, 128), 1) < WINS
    blank = jnp.zeros((WINS, 128), F32)
    both = jnp.concatenate(
        [jnp.where(first, payload, 0.0), jnp.where(first, 0.0, payload)], axis=0
    )
    table = jnp.concatenate(
        [jnp.concatenate([both, blank], axis=0), jnp.concatenate([blank, both], axis=0)], axis=1
    )
    message = sum(dot_t(place, piece) for piece in split3(table))
    outbox[...] = message.reshape(N_TILE, 1, 128)

    mine = pltpu.make_async_copy(outbox.at[tile], inbox.at[tile], load_sem)
    mine.start()

    def box_copy(i):
        peer = lax.rem(tile + i, N_TILE)
        return pltpu.make_async_remote_copy(
            src_ref=outbox.at[peer],
            dst_ref=inbox.at[tile],
            send_sem=box_send,
            recv_sem=box_recv,
            device_id=(tm, peer),
            device_id_type=MESH,
        )

    def send_box(i, carry):
        box_copy(i).start()
        return carry

    lax.fori_loop(1, N_TILE, send_box, 0)
    mine.wait()
    others = pl.ds(0, N_TILE - 1)
    pltpu.make_async_copy(outbox.at[others], outbox.at[others], box_send).wait()
    pltpu.make_async_copy(inbox.at[others], inbox.at[others], box_recv).wait()
    got_ref[...] = inbox[...].reshape(N_TILE, 128)


def deposit(got_ref, out_ref):
    got = got_ref[...]
    slots = jnp.concatenate(
        [got] + [pltpu.roll(got, 128 - 32 * c, 1) for c in range(1, CAP)], axis=0
    )
    cells = slots[:, 24:25].astype(jnp.int32)
    dist = (iota((128, AZ), 1) - cells) & (AZ - 1)
    weights = jnp.zeros((128, AZ), F32)
    for k in range(SPREAD):
        weights = jnp.where(dist == k, slots[:, 16 + k : 17 + k], weights)
    w_hi, w_lo = split2(weights)
    across = slots.T
    values = across[0:16]
    band = across[24:25].astype(jnp.int32) // AZ
    lhs_hi, lhs_lo = split2(
        jnp.concatenate([jnp.where(band == r, values, 0.0) for r in range(4)], axis=0)
    )
    num = dot(lhs_hi, w_hi) + dot(lhs_lo, w_hi) + dot(lhs_hi, w_lo)
    for r in range(4):
        block = num[16 * r : 16 * r + 16]
        scale = 1.0 / jnp.maximum(block[6:7], 1.0)
        out_ref[0, :, r * AZ : (r + 1) * AZ] = block[0:6] * scale
        out_ref[1, :, r * AZ : (r + 1) * AZ] = block[8:14] * scale


def on_device(frames, peaks, calib, counts, owner, cell, spread, start):
    tables = [jnp.asarray(t) for t in _tables()]
    vmem, smem = pl.BlockSpec(memory_space=pltpu.VMEM), pl.BlockSpec(memory_space=pltpu.SMEM)
    hbm = pl.BlockSpec(memory_space=pl.ANY)
    width = frames.shape[3]
    got = pl.pallas_call(
        correlate_and_send,
        out_shape=jax.ShapeDtypeStruct((N_TILE, 128), F32),
        in_specs=[hbm] + [vmem] * 6 + [vmem, vmem, smem, vmem, vmem, vmem, smem],
        out_specs=vmem,
        scratch_shapes=[
            pltpu.VMEM((4, 128, width), BF),
            pltpu.VMEM((4, HALF, width), BF),
            pltpu.VMEM((4, HALF, width), BF),
            pltpu.VMEM((4, HALF, width), BF),
            pltpu.VMEM((16, width), F32),
            pltpu.VMEM((32, width), F32),
            pltpu.VMEM((N_TM, 8, 128), F32),
            pltpu.VMEM((N_TILE, 1, 128), F32),
            pltpu.VMEM((N_TILE, 1, 128), F32),
        ]
        + [pltpu.SemaphoreType.DMA] * 7,
        compiler_params=pltpu.CompilerParams(
            collective_id=0, has_side_effects=True, vmem_limit_bytes=40 * 1024 * 1024
        ),
    )(frames, *tables, peaks, calib, counts, owner, cell.reshape(1, -1), spread, start)
    return pl.pallas_call(
        deposit,
        out_shape=jax.ShapeDtypeStruct((2, 6, 4 * AZ), F32),
        in_specs=[vmem],
        out_specs=vmem,
    )(got)


def solution(mesh):
    return jax.shard_map(
        on_device,
        mesh=mesh,
        in_specs=(
            P("tm", None, "tile", None),
            P("tm", None, "tile"),
            P(None, "tile"),
            P("tile"),
            P("tile", None),
            P("tile"),
            P(None, "tile"),
            P(),
        ),
        out_specs=P("tm", None, "tile"),
        check_vma=False,
    )
```

profile of v0, /device:TPU:1, one launch (start us, length us, event | category | flops | bytes accessed | tf_op | source)
XLA Modules:
  0.0 43.8 jit_solution(14543697463168095941)
XLA Ops:
  0.0 0.0 copy-start.6
  1.3 0.0 copy-start.8
  1.3 0.0 copy-start.9
  1.3 0.0 copy-start.10
  1.3 0.0 copy-start.11
  1.3 0.8 %copy.15.owner = s32[64,1]{1,0:T(8,128)S(1)} copy(s32[64,1]{0,1:T(1,128)} %param.18) | data formatting | bytes 512 | tf_op args[4]
  2.1 0.0 copy-done.6
  2.1 0.0 copy-done.8
  2.1 0.0 copy-done.9
  2.1 0.0 copy-done.10
  2.1 0.0 copy-done.11
  2.2 0.0 copy-start
  2.2 1.2 %copy-done = bf16[1,4,128,1024]{3,2,1,0:T(8,128)(2,1)S(1)} copy-done((bf16[1,4,128,1024]{3,2,1,0:T(8,128)(2,1)S(1)}, bf16[1,4,128,1024]{3,2,1,0:T(8,128)(2,1)}, u32[]{:S(2)}) %copy-start) | copy-done | bytes 1048600
  3.4 0.0 copy-start.1
  3.4 0.9 %copy-done.1 = bf16[2,256,256]{2,1,0:T(8,128)(2,1)S(1)} copy-done((bf16[2,256,256]{2,1,0:T(8,128)(2,1)S(1)}, bf16[2,256,256]{2,1,0:T(8,128)(2,1)}, u32[]{:S(2)}) %copy-start.1) | copy-done | bytes 262168
  4.3 0.0 copy-start.2
  4.3 0.9 %copy-done.2 = bf16[2,256,256]{2,1,0:T(8,128)(2,1)S(1)} copy-done((bf16[2,256,256]{2,1,0:T(8,128)(2,1)S(1)}, bf16[2,256,256]{2,1,0:T(8,128)(2,1)}, u32[]{:S(2)}) %copy-start.2) | copy-done | bytes 262168
  5.3 0.0 copy-start.3
  5.3 0.9 %copy-done.3 = bf16[192,256]{1,0:T(8,128)(2,1)S(1)} copy-done((bf16[192,256]{1,0:T(8,128)(2,1)S(1)}, bf16[192,256]{1,0:T(8,128)(2,1)}, u32[]{:S(2)}) %copy-start.3) | copy-done | bytes 98328
  6.2 0.0 copy-start.5
  6.2 0.8 %copy-done.5 = bf16[192,128]{1,0:T(8,128)(2,1)S(1)} copy-done((bf16[192,128]{1,0:T(8,128)(2,1)S(1)}, bf16[192,128]{1,0:T(8,128)(2,1)}, u32[]{:S(2)}) %copy-start.5) | copy-done | bytes 49176
  7.0 0.0 copy-start.7
  7.0 0.8 %copy-done.7 = bf16[64,192]{1,0:T(8,128)(2,1)S(1)} copy-done((bf16[64,192]{1,0:T(8,128)(2,1)S(1)}, bf16[64,192]{1,0:T(8,128)(2,1)}, u32[]{:S(2)}) %copy-start.7) | copy-done | bytes 24600
  7.7 31.9 %shard_map.136.got_ref = f32[32,128]{1,0:T(8,128)S(1)} custom-call(bf16[1,4,128,1024]{3,2,1,0:T(8,128)(2,1)S(1)} %copy-done, bf16[2,256,256]{2,1,0:T(8,128)(2,1)S(1)} %copy-done.2, bf16[2,256,256]{2,1,0:T(8,128)(2,1)S(1)} %copy-done.1, bf16[192,256]{1,0:T(8,128)(2,1)S(1)} %copy-done.3, bf16[192,128]{1,0:T(8,128)(2,1)S(1)} %copy-done.5, ...), custom_call_target="tpu_custom_call" | custom-call | tf_op jit(solution)/shard_map/pallas_call | solution.py:414
  39.6 0.0 copy-start.4
  39.6 0.6 %copy-done.4 = f32[32,128]{1,0:T(8,128)} copy-done((f32[32,128]{1,0:T(8,128)}, f32[32,128]{1,0:T(8,128)S(1)}, u32[]{:S(2)}) %copy-start.4) | copy-done | bytes 16408
  40.2 1.9 %shard_map.137 = f32[2,6,2048]{2,1,0:T(8,128)} custom-call(f32[32,128]{1,0:T(8,128)} %copy-done.4), custom_call_target="tpu_custom_call" | custom-call | tf_op jit(solution)/shard_map/pallas_call | solution.py:435
  42.1 1.6 %copy.16 = f32[2,6,2048]{2,0,1:T(2,128)} copy(f32[2,6,2048]{2,1,0:T(8,128)} %shard_map.137) | data formatting | bytes 196608 | tf_op jit(solution)/shard_map/pallas_call | solution.py:435
Async XLA Ops:
  0.0 2.1 %copy-start.6 = (bf16[64,192]{1,0:T(8,128)(2,1)S(1)}, bf16[64,192]{1,0:T(8,128)(2,1)}, u32[]{:S(2)}) copy-start(bf16[64,192]{1,0:T(8,128)(2,1)} %constant.17.clone.iy) | copy-start | bytes 73732
  1.3 0.8 %copy-start.8 = (f32[12,64]{1,0:T(8,128)S(1)}, f32[12,64]{1,0:T(8,128)}, u32[]{:S(2)}) copy-start(f32[12,64]{1,0:T(8,128)} %calib.1) | copy-start | bytes 9220
  1.3 0.8 %copy-start.9 = (f32[8,64]{1,0:T(8,128)S(1)}, f32[8,64]{1,0:T(8,128)}, u32[]{:S(2)}) copy-start(f32[8,64]{1,0:T(8,128)} %spread.1) | copy-start | bytes 6148
  1.3 0.8 %copy-start.10 = (s32[1,4,64]{2,1,0:T(4,128)S(1)}, s32[1,4,64]{2,1,0:T(4,128)}, u32[]{:S(2)}) copy-start(s32[1,4,64]{2,1,0:T(4,128)} %peaks.1) | copy-start | bytes 3076
  1.3 0.8 %copy-start.11 = (s32[64]{0:T(128)S(1)}, s32[64]{0:T(128)}, u32[]{:S(2)}) copy-start(s32[64]{0:T(128)} %param.19) | copy-start | bytes 772
  2.2 1.2 %copy-start = (bf16[1,4,128,1024]{3,2,1,0:T(8,128)(2,1)S(1)}, bf16[1,4,128,1024]{3,2,1,0:T(8,128)(2,1)}, u32[]{:S(2)}) copy-start(bf16[1,4,128,1024]{3,2,1,0:T(8,128)(2,1)} %frames.1) | copy-start | bytes 3145732
  3.4 0.9 %copy-start.1 = (bf16[2,256,256]{2,1,0:T(8,128)(2,1)S(1)}, bf16[2,256,256]{2,1,0:T(8,128)(2,1)}, u32[]{:S(2)}) copy-start(bf16[2,256,256]{2,1,0:T(8,128)(2,1)} %constant.13.clone.ix) | copy-start | bytes 786436
  4.3 0.9 %copy-start.2 = (bf16[2,256,256]{2,1,0:T(8,128)(2,1)S(1)}, bf16[2,256,256]{2,1,0:T(8,128)(2,1)}, u32[]{:S(2)}) copy-start(bf16[2,256,256]{2,1,0:T(8,128)(2,1)} %constant.12.clone.fx) | copy-start | bytes 786436
  5.3 0.9 %copy-start.3 = (bf16[192,256]{1,0:T(8,128)(2,1)S(1)}, bf16[192,256]{1,0:T(8,128)(2,1)}, u32[]{:S(2)}) copy-start(bf16[192,256]{1,0:T(8,128)(2,1)} %constant.14.clone.fy2) | copy-start | bytes 294916
  6.2 0.8 %copy-start.5 = (bf16[192,128]{1,0:T(8,128)(2,1)S(1)}, bf16[192,128]{1,0:T(8,128)(2,1)}, u32[]{:S(2)}) copy-start(bf16[192,128]{1,0:T(8,128)(2,1)} %constant.15.clone.fy_lo) | copy-start | bytes 147460
  7.0 0.8 %copy-start.7 = (bf16[64,192]{1,0:T(8,128)(2,1)S(1)}, bf16[64,192]{1,0:T(8,128)(2,1)}, u32[]{:S(2)}) copy-start(bf16[64,192]{1,0:T(8,128)(2,1)} %constant.16.clone.fyb) | copy-start | bytes 73732
  39.6 0.6 %copy-start.4 = (f32[32,128]{1,0:T(8,128)}, f32[32,128]{1,0:T(8,128)S(1)}, u32[]{:S(2)}) copy-start(f32[32,128]{1,0:T(8,128)S(1)} %shard_map.136.got_ref) | copy-start | bytes 49156
where the time goes:
time: 44.3 us; the launch traced here: 43.8 us
  Pallas kernels  33.8 us (76%)
  local copies, waits for them, and re-layouts  8.58 us (19%)
  between operations  1.4 us (3%)
    pallas_call x1, Pallas kernels, on_device(): pl.pallas_call(correlate_and_send, out_shape=jax.ShapeDtypeStruct((N_TILE...  31.9 us
    unnamed x25, local copies, waits for them, and re-layouts  6.95 us
    pallas_call x1, Pallas kernels, on_device(): pl.pallas_call(deposit, out_shape=jax.ShapeDtypeStruct((2, 6, 4 * AZ), F3...  1.92 us
    pallas_call x1, local copies, waits for them, and re-layouts, on_device(): pl.pallas_call(deposit, out_shape=jax.ShapeDtypeStruct((2, 6, 4 * AZ), F3...  1.62 us

commit v1 on v0

--- a/solution.py
+++ b/solution.py
@@ -147,16 +147,25 @@
 
 
 def correlate_and_send(
-    frames, fx, ix, fy2, fy_lo, fyb, iy, peaks, calib, counts, owner, cell, spread, start,
-    got_ref,
-    image, halo, edge_hi, edge_lo, peak_lanes, stats, vecs, outbox, inbox,
-    load_sem, halo_send, halo_recv, vec_send, vec_recv, box_send, box_recv,
+    frames, *refs,
 ):
+    hbm_inputs, got_ref, inputs = refs[:12], refs[12], refs[13:25]
+    fx, ix, fy2, fy_lo, fyb, iy, peaks, calib, scalars, owner, cell, spread = inputs
+    image, halo, edge_hi, edge_lo, peak_lanes, stats, vecs, outbox, inbox = refs[25:34]
+    load_sem, halo_send, halo_recv, vec_send, vec_recv, box_send, box_recv, input_sems = refs[34:]
     tm, tile = lax.axis_index("tm"), lax.axis_index("tile")
     above, below = lax.rem(tile + N_TILE - 1, N_TILE), lax.rem(tile + 1, N_TILE)
 
+    loads = [
+        pltpu.make_async_copy(source, target, input_sems.at[i])
+        for i, (source, target) in enumerate(zip(hbm_inputs, inputs))
+    ]
     load = pltpu.make_async_copy(frames.at[0], image, load_sem)
+    for one in loads[6:]:
+        one.start()
     load.start()
+    for one in loads[:6]:
+        one.start()
 
     barrier = pltpu.get_barrier_semaphore()
 
@@ -174,6 +183,9 @@
 
     lax.fori_loop(1, N_TM, greet_tm, 0)
     lax.fori_loop(1, N_TILE, greet_tile, 0)
+
+    for one in loads[6:]:
+        one.wait()
 
     stats[...] = jnp.zeros_like(stats)
     peak = peaks[0].astype(F32)
@@ -189,15 +201,21 @@
     peak_lanes[...] = dot(picks, to_lanes)
 
     pl.semaphore_wait(barrier, N_TM + N_TILE - 2)
-    halo_copy = pltpu.make_async_remote_copy(
-        src_ref=frames.at[0, :, pl.ds(0, HALF), :],
-        dst_ref=halo,
-        send_sem=halo_send,
-        recv_sem=halo_recv,
-        device_id=(tm, above),
-        device_id_type=MESH,
-    )
-    halo_copy.start()
+    def halo_copy(g):
+        lanes = pl.ds(g * GROUP, GROUP)
+        return pltpu.make_async_remote_copy(
+            src_ref=frames.at[0, :, pl.ds(0, HALF), lanes],
+            dst_ref=halo.at[:, :, lanes],
+            send_sem=halo_send.at[g],
+            recv_sem=halo_recv.at[g],
+            device_id=(tm, above),
+            device_id_type=MESH,
+        )
+
+    for g in range(4):
+        halo_copy(g).start()
+    for one in loads[:6]:
+        one.wait()
     load.wait()
 
     weight = jnp.where(iota((HALF, 128), 0) == 0, 1.0, 2.0) * jnp.where(
@@ -257,12 +275,12 @@
         correlate(t, 3, 0, lanes, GROUP)
         return carry
 
-    lax.fori_loop(0, 4, own_bands, 0)
-
-    halo_copy.wait()
+    lax.fori_loop(0, 4, own_bands, 0, unroll=True)
+
 
     def last_band(g, carry):
-        lanes = pl.multiple_of(g * GROUP, GROUP)
+        halo_copy(g).wait()
+        lanes = g * GROUP
         pixels = halo[:, :, pl.ds(lanes, GROUP)].reshape(4 * HALF, GROUP)
         x = dot(pixels, fx[0]) + dot(pixels, fx[1])
         x_hi, x_lo = split2(jnp.where(tile == N_TILE - 1, 0.0, x))
@@ -274,7 +292,8 @@
         correlate(t, 1, 3, lanes, GROUP)
         return carry
 
-    lax.fori_loop(0, 4, last_band, 0)
+    for g in range(4):
+        last_band(g, 0)
 
     lane = iota((8, 128), 1)
     window = lane % WINS
@@ -290,12 +309,13 @@
         for part in range(2):
             j, i = 2 * cam + part, 2 + 2 * part + cam
             disp.append(peak2[j : j + 1] + y[i : i + 1] * inverse[cam : cam + 1])
-    live = (window >= WINS - counts[0]).astype(F32)
+    live = (window >= WINS - scalars[:, 0:1]).astype(F32)
     calib2 = jnp.concatenate([calib[...], calib[...]], axis=1)
     vec = []
     for i in range(3):
         vec.append(sum(calib2[4 * i + j : 4 * i + j + 1] * disp[j] for j in range(4)))
-    six = jnp.concatenate(vec + vec + [jnp.zeros((2, 128), F32)], axis=0) * live
+        vec.append(vec[-1])
+    six = jnp.concatenate(vec + [jnp.zeros((2, 128), F32)], axis=0) * live
     vecs[pl.ds(tm, 1)] = six[None]
 
     def vec_copy(i):
@@ -312,9 +332,8 @@
     for i in range(1, N_TM):
         vec_copy(i).start()
 
-    owners = jnp.concatenate([owner[...], owner[...]], axis=0)
-    named = (owners == iota((128, 128), 1)).astype(F32)
-    hits = named.T[0:N_TILE]
+    owners = jnp.concatenate([owner[...], owner[...]], axis=1)
+    hits = (owners == iota((N_TILE, 128), 0)).astype(F32)
     before = ((iota((128, 128), 0) < iota((128, 128), 1) % WINS) & (iota((128, 128), 0) < WINS))
     earlier = dot(hits.astype(BF), before.astype(F32).astype(BF))
     rank = jnp.sum(hits * earlier, axis=0, keepdims=True)
@@ -326,12 +345,11 @@
     cells = jnp.broadcast_to(jnp.concatenate([cells, cells], axis=1), (8, 128))
     spread2 = jnp.concatenate([spread[...], spread[...]], axis=1) * live
     part = iota((8, 128), 0)
-    turn = jnp.where(part >= 3, 4, 0)
+    freq = tm * 2 + (part & 1)
     coefs = []
     for k in range(2):
-        freq = tm * 2 + k
         for s in range(N_TM):
-            n = (freq * (start[0] + s) + turn) & 15
+            n = (freq * (scalars[:, 1:2] + s) + 4 * k) & 15
             value = jnp.zeros((8, 128), F32)
             for step in range(16):
                 value = jnp.where(n == step, math.cos(2.0 * math.pi * step / 16), value)
@@ -402,21 +420,28 @@
     for r in range(4):
         block = num[16 * r : 16 * r + 16]
         scale = 1.0 / jnp.maximum(block[6:7], 1.0)
-        out_ref[0, :, r * AZ : (r + 1) * AZ] = block[0:6] * scale
-        out_ref[1, :, r * AZ : (r + 1) * AZ] = block[8:14] * scale
+        for k in range(2):
+            terms = (block[8 * k : 8 * k + 6] * scale).reshape(3, 2, AZ)
+            out_ref[3 * k : 3 * k + 3, :, r * AZ : (r + 1) * AZ] = terms
 
 
 def on_device(frames, peaks, calib, counts, owner, cell, spread, start):
     tables = [jnp.asarray(t) for t in _tables()]
-    vmem, smem = pl.BlockSpec(memory_space=pltpu.VMEM), pl.BlockSpec(memory_space=pltpu.SMEM)
-    hbm = pl.BlockSpec(memory_space=pl.ANY)
+    vmem, hbm = pl.BlockSpec(memory_space=pltpu.VMEM), pl.BlockSpec(memory_space=pltpu.HBM)
     width = frames.shape[3]
+    inputs = (
+        *tables, peaks, calib, jnp.concatenate([counts, start]).reshape(1, 2), owner.reshape(1, -1),
+        cell.reshape(1, -1), spread,
+    )
     got = pl.pallas_call(
         correlate_and_send,
         out_shape=jax.ShapeDtypeStruct((N_TILE, 128), F32),
-        in_specs=[hbm] + [vmem] * 6 + [vmem, vmem, smem, vmem, vmem, vmem, smem],
+        in_specs=[hbm] * 13,
         out_specs=vmem,
         scratch_shapes=[
+            pltpu.VMEM(x.shape, x.dtype) for x in inputs
+        ]
+        + [
             pltpu.VMEM((4, 128, width), BF),
             pltpu.VMEM((4, HALF, width), BF),
             pltpu.VMEM((4, HALF, width), BF),
@@ -427,17 +452,21 @@
             pltpu.VMEM((N_TILE, 1, 128), F32),
             pltpu.VMEM((N_TILE, 1, 128), F32),
         ]
-        + [pltpu.SemaphoreType.DMA] * 7,
+        + [pltpu.SemaphoreType.DMA, pltpu.SemaphoreType.DMA((4,)), pltpu.SemaphoreType.DMA((4,))]
+        + [pltpu.SemaphoreType.DMA] * 4
+        + [pltpu.SemaphoreType.DMA((12,))],
         compiler_params=pltpu.CompilerParams(
-            collective_id=0, has_side_effects=True, vmem_limit_bytes=40 * 1024 * 1024
+            collective_id=0, has_side_effects=True, vmem_limit_bytes=63 * 1024 * 1024
         ),
-    )(frames, *tables, peaks, calib, counts, owner, cell.reshape(1, -1), spread, start)
-    return pl.pallas_call(
+    )(frames, *inputs)
+    spectrum = pl.pallas_call(
         deposit,
-        out_shape=jax.ShapeDtypeStruct((2, 6, 4 * AZ), F32),
+        out_shape=jax.ShapeDtypeStruct((6, 2, 4 * AZ), F32),
         in_specs=[vmem],
         out_specs=vmem,
+        compiler_params=pltpu.CompilerParams(vmem_limit_bytes=63 * 1024 * 1024),
     )(got)
+    return spectrum.transpose(1, 0, 2)
 
 
 def solution(mesh):

time: 44.3 us -> 34.4 us (0.78)
  local copies, waits for them, and re-layouts: 8.58 us -> 0 us
  Pallas kernels: 33.8 us -> 32.3 us
  other arithmetic: 0 us -> 0.59 us
    unnamed x25 -> x0, local copies, waits for them, and re-layouts: 6.95 us -> none
    pallas_call x1 -> x0, local copies, waits for them, and re-layouts: 1.62 us -> none  [on_device(): pl.pallas_call(deposit, out_shape=jax.ShapeDtypeStruct((2, 6, 4 * AZ), F3...]
    pallas_call x1, Pallas kernels: 31.9 us -> 30.3 us  [on_device(): pl.pallas_call(correlate_and_send, out_shape=jax.ShapeDtypeStruct((N_TILE...]
    reshape x0 -> x1, other arithmetic: none -> 0.59 us  [on_device(): jnp.concatenate([counts, start]).reshape(1, 2)]
where the time goes in v1:
time: 34.4 us; the launch traced here: 34.2 us
  Pallas kernels  32.3 us (94%)
  between operations  1.31 us (4%)
  other arithmetic  0.59 us (2%)
    pallas_call x1, Pallas kernels, on_device(): pl.pallas_call(correlate_and_send, out_shape=jax.ShapeDtypeStruct((N_TILE...  30.3 us
    pallas_call x1, Pallas kernels, on_device(): pl.pallas_call(deposit, out_shape=jax.ShapeDtypeStruct((6, 2, 4 * AZ), F3...  1.94 us

profile of v1, /device:TPU:1, one launch (start us, length us, event | category | flops | bytes accessed | tf_op | source)
XLA Modules:
  0.0 34.2 jit_solution(11616535410381143485)
XLA Ops:
  1.3 0.6 %add_bitcast_fusion.refs_8_ = s32[1,2]{1,0:T(1,128)} fusion(s32[1]{0:T(128)S(6)} %copy.16, s32[1]{0:T(128)S(6)} %copy.15), kind=kLoop, calls=%fused_computation | loop fusion | flops 2 | bytes 16 | tf_op jit(solution)/shard_map/reshape | solution.py:433
  1.9 30.3 %shard_map.136.got_ref = f32[32,128]{1,0:T(8,128)} custom-call(bf16[1,4,128,1024]{3,2,1,0:T(8,128)(2,1)} %frames.1, bf16[2,256,256]{2,1,0:T(8,128)(2,1)} %constant.12.clone.refs_0_, bf16[2,256,256]{2,1,0:T(8,128)(2,1)} %constant.13.clone.refs_1_, bf16[192,256]{1,0:T(8,128)(2,1)} %constant.14.clone.refs_2_, bf16[192,128]{1,0:T(8,128)(2,1)} %constant.15.clone.refs_3_, ...), custom_call_target="tpu_custom_call" | custom-call | tf_op jit(solution)/shard_map/pallas_call | solution.py:436
  32.2 1.9 %shard_map.137 = f32[6,2,2048]{2,1,0:T(2,128)} custom-call(f32[32,128]{1,0:T(8,128)} %shard_map.136.got_ref), custom_call_target="tpu_custom_call" | custom-call | tf_op jit(solution)/shard_map/pallas_call | solution.py:462

commit v2 on v1

v2 whole, which is shorter than its diff:
```python
import itertools
import math

import jax
import jax.numpy as jnp
import ml_dtypes
import numpy as np
from jax import lax
from jax.experimental import pallas as pl
from jax.experimental.pallas import tpu as pltpu
from jax.sharding import PartitionSpec as P

WIN = 64
HALF = 32
FREQS = 16
NFFT = 4096
AZ = 512
SPREAD = 8
CAP = 4
GROUP = 256
WINS = 64
SHARPNESS = 20.0
MESH = pl.DeviceIdType.MESH
BF = jnp.bfloat16
F32 = jnp.float32
N_TM = 8
N_TILE = 32


def _pair(table):
    hi = table.astype(ml_dtypes.bfloat16)
    lo = (table - hi.astype(np.float64)).astype(ml_dtypes.bfloat16)
    return hi, lo


def _real_dft():
    n = np.arange(WIN)
    k = np.arange(HALF)[:, None]
    cos = np.round(np.cos(2.0 * np.pi * ((k * n) % WIN) / WIN), 14)
    sin = np.round(np.sin(2.0 * np.pi * ((k * n) % WIN) / WIN), 14)
    sin[0] = 1.0 - 2.0 * (n % 2)
    return cos, sin


def _tables():
    cos, sin = _real_dft()
    weight = np.where(np.arange(HALF) == 0, 1.0, 2.0)[:, None]
    eye = np.eye(4)
    fx = np.concatenate([np.kron(eye, cos.T), np.kron(eye, sin.T)], axis=1)
    ix = np.concatenate([np.kron(eye, weight * cos), np.kron(eye, weight * sin)], axis=0)
    fy = np.zeros((2, 3, HALF, 128))
    for r in range(3):
        fy[0, r, :, r * HALF : r * HALF + WIN] = cos
        fy[1, r, :, r * HALF : r * HALF + WIN] = sin
    fy = fy.reshape(192, 128)
    fyb = np.concatenate([cos, sin], axis=0)
    iy = np.concatenate([weight * cos, weight * sin], axis=0).T
    fx_hi, fx_lo = _pair(fx)
    ix_hi, ix_lo = _pair(ix)
    fy_hi, fy_lo = _pair(fy)
    fyb_hi, fyb_lo = _pair(fyb)
    iy_hi, iy_lo = _pair(iy)
    cat = np.concatenate
    return (
        np.stack([fx_hi, fx_lo]),
        np.stack([ix_hi, ix_lo]),
        cat([fy_hi, fy_hi], axis=1),
        fy_lo,
        cat([fyb_hi, fyb_hi, fyb_lo], axis=1),
        cat([iy_hi, iy_hi, iy_lo], axis=1),
    )


def dot(lhs, rhs):
    return jnp.dot(lhs, rhs, preferred_element_type=F32)


def dot_t(lhs, rhs):
    return lax.dot_general(lhs, rhs, (((1,), (1,)), ((), ())), preferred_element_type=F32)


def split2(x):
    hi = x.astype(BF)
    return hi, (x - hi.astype(F32)).astype(BF)


def split3(x):
    hi = x.astype(BF)
    rest = x - hi.astype(F32)
    mid = rest.astype(BF)
    return hi, mid, (rest - mid.astype(F32)).astype(BF)


def iota(shape, dim):
    return lax.broadcasted_iota(jnp.int32, shape, dim)


def cross(first, second, y0, x0):
    a, b, c, d = first
    a2, b2, c2, d2 = second
    aa, bb, cc, dd = a * a2, b * b2, c * c2, d * d2
    ac, bd = a * c2 - c * a2, b * d2 - d * b2
    ab, cd = a * b2 - b * a2, c * d2 - d * c2
    ad, bc = a * d2 + d * a2, b * c2 + c * b2
    low, high = jnp.where(x0, aa, aa + cc), jnp.where(x0, bb, bb + dd)
    low_s, high_s = jnp.where(x0, cc, ac), jnp.where(x0, dd, bd)
    p_cc = jnp.where(y0, low, low + high)
    p_cs = jnp.where(y0, low_s, jnp.where(x0, cc + dd, ac + bd))
    p_sc = jnp.where(y0, high, jnp.where(x0, ab, ab + cd))
    p_ss = jnp.where(y0, high_s, jnp.where(x0, cd, ad - bc))
    return p_cc, p_cs, p_sc, p_ss


def parts(t, half):
    return t[:half, :128], t[half:, :128], t[:half, 128:], t[half:, 128:]


def inverse_x(spectra, ix):
    rows = []
    for p_cc, p_cs, p_sc, p_ss in spectra:
        rows.append(jnp.concatenate([p_cc, p_cs], axis=1))
        rows.append(jnp.concatenate([p_sc, p_ss], axis=1))
    hi, lo = split2(jnp.concatenate(rows, axis=0))
    return dot(hi, ix[0]) + dot(lo, ix[0]) + dot(hi, ix[1])


def energy_rows(four, weight, bands):
    a, b, c, d = four
    e = (a * a + b * b) + (c * c + d * d)
    return [
        jnp.sum(e[r * HALF : (r + 1) * HALF] * weight, axis=0, keepdims=True) for r in range(bands)
    ]


def inverse_norm(rows, spread_lanes):
    have = len(rows)
    padded = rows + [jnp.zeros((16 - have, 128), F32)] * (have < 16)
    hi, mid, lo = split3(jnp.concatenate(padded, axis=0))
    wide = dot(jnp.concatenate([hi, mid, lo], axis=0), spread_lanes)
    total = wide[0:16] + wide[16:32] + wide[32:48]
    return lax.rsqrt(total * (1.0 / 4096.0**2) + 1e-5)


def wrapped(lag, peak):
    off = lag - peak
    return jnp.where(off >= 32.0, off - 64.0, off)


def correlate_and_send(
    frames, *refs,
):
    hbm_inputs, got_ref, inputs = refs[:12], refs[12], refs[13:25]
    fx, ix, fy2, fy_lo, fyb, iy, peaks, calib, scalars, owner, cell, spread = inputs
    image, from_below, from_above, pack, pack_in, peak_lanes, stats, vecs, outbox, inbox = refs[25:35]
    load_sem, vec_send, vec_recv, box_send, box_recv, halo_send, halo_recv, input_sems, round_sem = (
        refs[35:]
    )
    tm, tile = lax.axis_index("tm"), lax.axis_index("tile")
    above, below = lax.rem(tile + N_TILE - 1, N_TILE), lax.rem(tile + 1, N_TILE)

    loads = [
        pltpu.make_async_copy(source, target, input_sems.at[i])
        for i, (source, target) in enumerate(zip(hbm_inputs, inputs))
    ]
    load = pltpu.make_async_copy(frames.at[0], image, load_sem)
    for one in loads[6:]:
        one.start()
    load.start()
    for one in loads[:6]:
        one.start()

    barrier = pltpu.get_barrier_semaphore()

    def greet(sem, d_tm, d_tile):
        peer = (lax.rem(tm + d_tm, N_TM), lax.rem(tile + d_tile, N_TILE))
        pl.semaphore_signal(sem, 1, device_id=peer, device_id_type=MESH)

    near = [d % N_TILE for i in range(1, 9) for d in (i, -i)]
    for d in near:
        greet(barrier, 0, d)
    for d in range(1, N_TM):
        greet(barrier, d, 0)

    pl.semaphore_wait(barrier, len(near) + N_TM - 1)
    for d in (8, N_TILE - 8):
        greet(round_sem, 0, d)
    def to_tile(peer, source, target, i):
        return pltpu.make_async_remote_copy(
            src_ref=source,
            dst_ref=target,
            send_sem=halo_send.at[i],
            recv_sem=halo_recv.at[i],
            device_id=(tm, peer),
            device_id_type=MESH,
        )

    halos = [
        to_tile(above, frames.at[0, pl.ds(0, 2), pl.ds(0, HALF), :], from_below, 0),
        to_tile(below, frames.at[0, pl.ds(2, 2), pl.ds(96, HALF), :], from_above, 1),
        to_tile(below, pack, pack_in, 2),
    ]
    halos[0].start()
    halos[1].start()
    for one in loads[6:]:
        one.wait()

    def twice(x):
        return jnp.concatenate([x, x], axis=1)

    window = iota((8, 128), 1) % WINS
    live = (window >= WINS - scalars[:, 0:1]).astype(F32)
    peak2, calib2 = twice(peaks[0].astype(F32)), twice(calib[...])
    owner2 = twice(owner[...].astype(F32))
    pack[0:16] = jnp.concatenate([calib2, peak2], axis=0)
    pack[16:24] = jnp.concatenate([owner2, live[0:7]], axis=0)
    halos[2].start()

    stats[...] = jnp.zeros_like(stats)
    band_of = iota((4, WINS), 1) // 16
    to_lanes = (iota((WINS, 1024), 0) % 16 == iota((WINS, 1024), 1) // WIN).astype(F32).astype(BF)

    def lanes_of_peaks(peak):
        picks = [
            jnp.where(
                iota((4, WINS), 0) == band_of, jnp.broadcast_to(peak[j : j + 1, :WINS], (4, WINS)), 0.0
            )
            for j in range(4)
        ]
        return dot(jnp.concatenate(picks, axis=0).astype(BF), to_lanes)

    peak_lanes[0:16] = lanes_of_peaks(peak2)

    for one in loads[:6]:
        one.wait()
    load.wait()

    weight = jnp.where(iota((HALF, 128), 0) == 0, 1.0, 2.0) * jnp.where(
        iota((HALF, 128), 1) % HALF == 0, 1.0, 2.0
    )
    spread_lanes = (iota((128, GROUP), 0) // HALF == iota((128, GROUP), 1) // WIN).astype(F32)
    spread_lanes = spread_lanes.astype(BF)
    row_lag = iota((WIN, GROUP), 0).astype(F32)
    col_lag = (iota((1, GROUP), 1) % WIN).astype(F32)
    gain = SHARPNESS * math.log2(math.e) / 4096.0**2

    def slots(bands):
        shape = (bands * HALF, 128)
        y0, x0 = iota(shape, 0) % HALF == 0, iota(shape, 1) % HALF == 0
        return y0, x0, y0 & x0

    def correlate(ts, bands, at_lanes, at_stats):
        half = bands * HALF
        y0, x0, dc = slots(bands)
        scales, spectra = [], []
        for t in ts:
            four = []
            for one in t:
                a, b, c, d = parts(one, half)
                four.append((jnp.where(dc, 0.0, a), b, c, d))
            energies = [row for one in four for row in energy_rows(one, weight, bands)]
            scales.append(inverse_norm(energies, spread_lanes))
            spectra += [cross(four[2 * cam], four[2 * cam + 1], y0, x0) for cam in range(2)]
        z_hi, z_lo = split2(inverse_x(spectra, ix))
        for g, cam, r in itertools.product(range(len(ts)), range(2), range(bands)):
            lanes, scale = slice(g * GROUP, (g + 1) * GROUP), scales[g]
            at = [((g * 2 + cam) * 2 + part) * half + r * HALF for part in range(2)]
            hi = [z_hi[i : i + HALF] for i in at]
            lo = [z_lo[i : i + HALF] for i in at]
            corr = dot(iy[...], jnp.concatenate(hi + lo + hi, axis=0))
            i, j = (2 * cam) * bands + r, (2 * cam + 1) * bands + r
            p = jnp.exp2(corr * (scale[i : i + 1] * scale[j : j + 1] * gain))
            i = at_lanes(cam, r)
            rows_at, cols_at = peak_lanes[i : i + 1, lanes], peak_lanes[i + 4 : i + 5, lanes]
            total = jnp.sum(p, axis=0, keepdims=True)
            by_row = jnp.sum(p * wrapped(row_lag, rows_at), axis=0, keepdims=True)
            by_col = total * wrapped(col_lag, cols_at)
            for k, value in enumerate((total, by_row, by_col)):
                i = at_stats(cam, r) * 8 + k * 2 + cam
                stats[i : i + 1, lanes] = value

    def x_transform(blocks):
        rows = [block[:, g * GROUP : (g + 1) * GROUP] for g in range(4) for block in blocks]
        pixels = jnp.concatenate(rows, axis=0)
        return dot(pixels, fx[0]) + dot(pixels, fx[1])

    x_hi, x_lo = split2(x_transform([image[f] for f in range(4)]))
    ts, edges = [], []
    for g in range(4):
        t = []
        for f in range(4):
            at = (g * 4 + f) * 128
            hi, lo = x_hi[at : at + 128], x_lo[at : at + 128]
            edges.append((hi[96:], lo[96:]) if f < 2 else (hi[:HALF], lo[:HALF]))
            t.append(dot(fy2[...], jnp.concatenate([hi, lo], axis=0)) + dot(fy_lo[...], hi))
        ts.append(t)
    correlate(ts, 3, lambda cam, r: 8 * cam + r, lambda cam, r: r)

    to_window = (iota((1024, 128), 0) // WIN == iota((1024, 128), 1) % 16).astype(F32).astype(BF)
    before = (iota((128, 128), 0) < iota((128, 128), 1) % WINS) & (iota((128, 128), 0) < WINS)
    before = before.astype(F32).astype(BF)
    half = (iota((1, 128), 1) // WINS).astype(F32)

    def places(owners):
        hits = (owners.astype(jnp.int32) == iota((N_TILE, 128), 0)).astype(F32)
        rank = jnp.sum(hits * dot(hits.astype(BF), before), axis=0, keepdims=True)
        both = [jnp.where(rank == half, hits, 0.0), jnp.where(rank == half + 2.0, hits, 0.0)]
        return jnp.concatenate(both, axis=1).astype(BF)

    place = places(owner2)
    cells = jnp.broadcast_to(twice(cell[...].astype(F32)), (8, 128))
    spread2 = twice(spread[...]) * live
    freq = tm * 2 + (iota((8, 128), 0) & 1)
    coefs = []
    for k in range(2):
        for s in range(N_TM):
            n = (freq * (scalars[:, 1:2] + s) + 4 * k) & 15
            value = jnp.zeros((8, 128), F32)
            for step in range(16):
                value = jnp.where(n == step, math.cos(2.0 * math.pi * step / 16), value)
            coefs.append(value)

    halos[2].wait()
    place_above = places(pack_in[16:17])
    peak_above, calib_above, live_above = pack_in[12:16], pack_in[0:12], pack_in[17:18]
    peak_lanes[16:32] = lanes_of_peaks(peak_above)

    halos[0].wait()
    halos[1].wait()
    x_hi, x_lo = split2(
        x_transform([from_below[0], from_below[1], from_above[0], from_above[1]])
    )
    last, first = tile == N_TILE - 1, tile == 0
    ts = []
    for g in range(4):
        t = []
        for f in range(4):
            at = (g * 4 + f) * HALF
            there = [x_hi[at : at + HALF], x_lo[at : at + HALF]]
            here = edges[g * 4 + f]
            if f < 2:
                there = [jnp.where(last, 0.0, x.astype(F32)).astype(BF) for x in there]
                hi, lo = [[a, b] for a, b in zip(here, there)]
            else:
                here = [jnp.where(first, 0.0, x.astype(F32)).astype(BF) for x in here]
                hi, lo = [[a, b] for a, b in zip(there, here)]
            t.append(dot(fyb[...], jnp.concatenate(hi + lo + hi, axis=0)))
        ts.append(t)
    correlate(ts, 1, lambda cam, r: 3 + 24 * cam, lambda cam, r: 3 + cam)

    hi, mid, lo = split3(stats[...])
    y = dot(jnp.concatenate([hi, mid, lo], axis=0), to_window)
    y = y[0:40] + y[40:80] + y[80:120]
    across = window[0:1] >= 48
    y_above = y[32:40]
    y = sum(jnp.where(window // 16 == r, y[8 * r : 8 * r + 8], 0.0) for r in range(4))

    def displacement(y, peak, cam):
        inverse = 1.0 / y[cam : cam + 1]
        return [
            peak[2 * cam + part : 2 * cam + part + 1]
            + y[2 + 2 * part + cam : 3 + 2 * part + cam] * inverse
            for part in range(2)
        ]

    def six_rows(calib, disp, live):
        vec = []
        for i in range(3):
            vec.append(sum(calib[4 * i + j : 4 * i + j + 1] * d for j, d in disp) * live)
            vec.append(vec[-1])
        return jnp.concatenate(vec + [jnp.zeros((2, 128), F32)], axis=0)

    disp = displacement(y, peak2, 0)
    disp += [jnp.where(across, 0.0, d) for d in displacement(y, peak2, 1)]
    own = six_rows(calib2, list(enumerate(disp)), live[0:1])
    disp = displacement(y_above, peak_above, 1)
    other = six_rows(calib_above, list(enumerate(disp, 2)), jnp.where(across, live_above, 0.0))
    vecs[pl.ds(tm, 1)] = jnp.concatenate([own, other], axis=0)[None]

    def vec_copy(i):
        peer = lax.rem(tm + i, N_TM)
        return pltpu.make_async_remote_copy(
            src_ref=vecs.at[tm],
            dst_ref=vecs.at[tm],
            send_sem=vec_send,
            recv_sem=vec_recv,
            device_id=(peer, tile),
            device_id_type=MESH,
        )

    for i in range(1, N_TM):
        vec_copy(i).start()

    pltpu.make_async_copy(vecs.at[pl.ds(0, 7)], vecs.at[pl.ds(0, 7)], vec_send).wait()
    pl.semaphore_wait(round_sem, 2)
    pltpu.make_async_copy(vecs.at[pl.ds(0, 7)], vecs.at[pl.ds(0, 7)], vec_recv).wait()
    def summed(k, rows):
        return sum(coefs[k * N_TM + s] * vecs[s, rows] for s in range(N_TM))

    first = iota((32, 128), 1) < WINS
    blank = jnp.zeros((WINS, 128), F32)

    def message(place, payload):
        both = jnp.concatenate(
            [jnp.where(first, payload, 0.0), jnp.where(first, 0.0, payload)], axis=0
        )
        table = jnp.concatenate(
            [jnp.concatenate([both, blank], axis=0), jnp.concatenate([blank, both], axis=0)], axis=1
        )
        return sum(dot_t(place, piece) for piece in split3(table))

    own, other = slice(0, 8), slice(8, 16)
    payload = jnp.concatenate([summed(0, own), summed(1, own), spread2, cells], axis=0)
    payload_above = jnp.concatenate(
        [summed(0, other), summed(1, other), jnp.zeros((16, 128), F32)], axis=0
    )
    outbox[:, 0:1] = message(place, payload).reshape(N_TILE, 1, 128)
    outbox[:, 1:2] = message(place_above, payload_above).reshape(N_TILE, 1, 128)

    mine = pltpu.make_async_copy(outbox.at[tile], inbox.at[tile], load_sem)
    mine.start()

    def box_copy(i):
        peer = lax.rem(tile + i, N_TILE)
        return pltpu.make_async_remote_copy(
            src_ref=outbox.at[peer],
            dst_ref=inbox.at[tile],
            send_sem=box_send,
            recv_sem=box_recv,
            device_id=(tm, peer),
            device_id_type=MESH,
        )

    def send_box(i, carry):
        box_copy(i).start()
        return carry

    lax.fori_loop(1, N_TILE, send_box, 0)
    mine.wait()
    others = pl.ds(0, N_TILE - 1)
    pltpu.make_async_copy(outbox.at[others], outbox.at[others], box_send).wait()
    pltpu.make_async_copy(inbox.at[others], inbox.at[others], box_recv).wait()
    first, second = inbox[:, 0], inbox[:, 1]
    got_ref[...] = first + jnp.concatenate([second[1:], second[:1]], axis=0)


def deposit(got_ref, out_ref):
    got = got_ref[...]
    slots = jnp.concatenate(
        [got] + [pltpu.roll(got, 128 - 32 * c, 1) for c in range(1, CAP)], axis=0
    )
    cells = slots[:, 24:25].astype(jnp.int32)
    dist = (iota((128, AZ), 1) - cells) & (AZ - 1)
    weights = jnp.zeros((128, AZ), F32)
    for k in range(SPREAD):
        weights = jnp.where(dist == k, slots[:, 16 + k : 17 + k], weights)
    w_hi, w_lo = split2(weights)
    across = slots.T
    values = jnp.where(iota((16, 128), 0) == 6, 1.0, across[0:16])
    band = across[24:25].astype(jnp.int32) // AZ
    lhs_hi, lhs_lo = split2(
        jnp.concatenate([jnp.where(band == r, values, 0.0) for r in range(4)], axis=0)
    )
    num = dot(lhs_hi, w_hi) + dot(lhs_lo, w_hi) + dot(lhs_hi, w_lo)
    for r in range(4):
        block = num[16 * r : 16 * r + 16]
        scale = 1.0 / jnp.maximum(block[6:7], 1.0)
        for k in range(2):
            terms = (block[8 * k : 8 * k + 6] * scale).reshape(3, 2, AZ)
            out_ref[3 * k : 3 * k + 3, :, r * AZ : (r + 1) * AZ] = terms


def on_device(frames, peaks, calib, counts, owner, cell, spread, start):
    tables = [jnp.asarray(t) for t in _tables()]
    vmem, hbm = pl.BlockSpec(memory_space=pltpu.VMEM), pl.BlockSpec(memory_space=pltpu.HBM)
    width = frames.shape[3]
    inputs = (
        *tables, peaks, calib, jnp.concatenate([counts, start]).reshape(1, 2), owner.reshape(1, -1),
        cell.reshape(1, -1), spread,
    )
    got = pl.pallas_call(
        correlate_and_send,
        out_shape=jax.ShapeDtypeStruct((N_TILE, 128), F32),
        in_specs=[hbm] * 13,
        out_specs=vmem,
        scratch_shapes=[
            pltpu.VMEM(x.shape, x.dtype) for x in inputs
        ]
        + [
            pltpu.VMEM((4, 128, width), BF),
            pltpu.VMEM((2, HALF, width), BF),
            pltpu.VMEM((2, HALF, width), BF),
            pltpu.VMEM((24, 128), F32),
            pltpu.VMEM((24, 128), F32),
            pltpu.VMEM((32, width), F32),
            pltpu.VMEM((40, width), F32),
            pltpu.VMEM((N_TM, 16, 128), F32),
            pltpu.VMEM((N_TILE, 2, 128), F32),
            pltpu.VMEM((N_TILE, 2, 128), F32),
        ]
        + [pltpu.SemaphoreType.DMA] * 5
        + [pltpu.SemaphoreType.DMA((3,))] * 2
        + [pltpu.SemaphoreType.DMA((12,)), pltpu.SemaphoreType.REGULAR],
        compiler_params=pltpu.CompilerParams(
            collective_id=0, has_side_effects=True, vmem_limit_bytes=63 * 1024 * 1024
        ),
    )(frames, *inputs)
    spectrum = pl.pallas_call(
        deposit,
        out_shape=jax.ShapeDtypeStruct((6, 2, 4 * AZ), F32),
        in_specs=[vmem],
        out_specs=vmem,
        compiler_params=pltpu.CompilerParams(vmem_limit_bytes=63 * 1024 * 1024),
    )(got)
    return spectrum.transpose(1, 0, 2)


def solution(mesh):
    return jax.shard_map(
        on_device,
        mesh=mesh,
        in_specs=(
            P("tm", None, "tile", None),
            P("tm", None, "tile"),
            P(None, "tile"),
            P("tile"),
            P("tile", None),
            P("tile"),
            P(None, "tile"),
            P(),
        ),
        out_specs=P("tm", None, "tile"),
        check_vma=False,
    )
```

time: 34.4 us -> 32.2 us (0.936)
  Pallas kernels: 32.3 us -> 30.1 us
    pallas_call x1, Pallas kernels: 30.3 us -> 28.1 us  [on_device(): pl.pallas_call(correlate_and_send, out_shape=jax.ShapeDtypeStruct((N_TILE...]
where the time goes in v2:
time: 32.2 us; the launch traced here: 32 us
  Pallas kernels  30.1 us (93%)
  between operations  1.31 us (4%)
  other arithmetic  0.59 us (2%)
    pallas_call x1, Pallas kernels, on_device(): pl.pallas_call(correlate_and_send, out_shape=jax.ShapeDtypeStruct((N_TILE...  28.1 us
    pallas_call x1, Pallas kernels, on_device(): pl.pallas_call(deposit, out_shape=jax.ShapeDtypeStruct((6, 2, 4 * AZ), F3...  1.94 us

profile of v2, /device:TPU:1, one launch (start us, length us, event | category | flops | bytes accessed | tf_op | source)
XLA Modules:
  0.0 32.0 jit_solution(13358494114004514141)
XLA Ops:
  1.3 0.6 %add_bitcast_fusion.refs_8_ = s32[1,2]{1,0:T(1,128)} fusion(s32[1]{0:T(128)S(6)} %copy.16, s32[1]{0:T(128)S(6)} %copy.15), kind=kLoop, calls=%fused_computation | loop fusion | flops 2 | bytes 16 | tf_op jit(solution)/shard_map/reshape | solution.py:477
  1.9 28.1 %shard_map.136.got_ref = f32[32,128]{1,0:T(8,128)} custom-call(bf16[1,4,128,1024]{3,2,1,0:T(8,128)(2,1)} %frames.1, bf16[2,256,256]{2,1,0:T(8,128)(2,1)} %constant.12.clone.refs_0_, bf16[2,256,256]{2,1,0:T(8,128)(2,1)} %constant.13.clone.refs_1_, bf16[192,256]{1,0:T(8,128)(2,1)} %constant.14.clone.refs_2_, bf16[192,128]{1,0:T(8,128)(2,1)} %constant.15.clone.refs_3_, ...), custom_call_target="tpu_custom_call" | custom-call | tf_op jit(solution)/shard_map/pallas_call | solution.py:480
  30.0 1.9 %shard_map.137 = f32[6,2,2048]{2,1,0:T(2,128)} custom-call(f32[32,128]{1,0:T(8,128)} %shard_map.136.got_ref), custom_call_target="tpu_custom_call" | custom-call | tf_op jit(solution)/shard_map/pallas_call | solution.py:507

commit v3 on v2

--- a/solution.py
+++ b/solution.py
@@ -147,13 +147,13 @@
 
 
 def correlate_and_send(
-    frames, *refs,
+    counts, start, frames, *refs,
 ):
-    hbm_inputs, got_ref, inputs = refs[:12], refs[12], refs[13:25]
-    fx, ix, fy2, fy_lo, fyb, iy, peaks, calib, scalars, owner, cell, spread = inputs
-    image, from_below, from_above, pack, pack_in, peak_lanes, stats, vecs, outbox, inbox = refs[25:35]
+    hbm_inputs, got_ref, inputs = refs[:11], refs[11], refs[12:23]
+    fx, ix, fy2, fy_lo, fyb, iy, peaks, calib, owner, cell, spread = inputs
+    image, from_below, from_above, pack, pack_in, peak_lanes, stats, vecs, outbox, inbox = refs[23:33]
     load_sem, vec_send, vec_recv, box_send, box_recv, halo_send, halo_recv, input_sems, round_sem = (
-        refs[35:]
+        refs[33:]
     )
     tm, tile = lax.axis_index("tm"), lax.axis_index("tile")
     above, below = lax.rem(tile + N_TILE - 1, N_TILE), lax.rem(tile + 1, N_TILE)
@@ -208,7 +208,7 @@
         return jnp.concatenate([x, x], axis=1)
 
     window = iota((8, 128), 1) % WINS
-    live = (window >= WINS - scalars[:, 0:1]).astype(F32)
+    live = (window >= WINS - counts[0]).astype(F32)
     peak2, calib2 = twice(peaks[0].astype(F32)), twice(calib[...])
     owner2 = twice(owner[...].astype(F32))
     pack[0:16] = jnp.concatenate([calib2, peak2], axis=0)
@@ -313,7 +313,7 @@
     coefs = []
     for k in range(2):
         for s in range(N_TM):
-            n = (freq * (scalars[:, 1:2] + s) + 4 * k) & 15
+            n = (freq * (start[0] + s) + 4 * k) & 15
             value = jnp.zeros((8, 128), F32)
             for step in range(16):
                 value = jnp.where(n == step, math.cos(2.0 * math.pi * step / 16), value)
@@ -406,7 +406,7 @@
         table = jnp.concatenate(
             [jnp.concatenate([both, blank], axis=0), jnp.concatenate([blank, both], axis=0)], axis=1
         )
-        return sum(dot_t(place, piece) for piece in split3(table))
+        return sum(dot_t(place, piece) for piece in split2(table))
 
     own, other = slice(0, 8), slice(8, 16)
     payload = jnp.concatenate([summed(0, own), summed(1, own), spread2, cells], axis=0)
@@ -460,7 +460,9 @@
     lhs_hi, lhs_lo = split2(
         jnp.concatenate([jnp.where(band == r, values, 0.0) for r in range(4)], axis=0)
     )
-    num = dot(lhs_hi, w_hi) + dot(lhs_lo, w_hi) + dot(lhs_hi, w_lo)
+    num = dot(
+        jnp.concatenate([lhs_hi, lhs_hi], axis=1), jnp.concatenate([w_hi, w_lo], axis=0)
+    ) + dot(lhs_lo, w_hi)
     for r in range(4):
         block = num[16 * r : 16 * r + 16]
         scale = 1.0 / jnp.maximum(block[6:7], 1.0)
@@ -472,15 +474,15 @@
 def on_device(frames, peaks, calib, counts, owner, cell, spread, start):
     tables = [jnp.asarray(t) for t in _tables()]
     vmem, hbm = pl.BlockSpec(memory_space=pltpu.VMEM), pl.BlockSpec(memory_space=pltpu.HBM)
+    smem = pl.BlockSpec(memory_space=pltpu.SMEM)
     width = frames.shape[3]
     inputs = (
-        *tables, peaks, calib, jnp.concatenate([counts, start]).reshape(1, 2), owner.reshape(1, -1),
-        cell.reshape(1, -1), spread,
+        *tables, peaks, calib, owner.reshape(1, -1), cell.reshape(1, -1), spread
     )
     got = pl.pallas_call(
         correlate_and_send,
         out_shape=jax.ShapeDtypeStruct((N_TILE, 128), F32),
-        in_specs=[hbm] * 13,
+        in_specs=[smem, smem] + [hbm] * 12,
         out_specs=vmem,
         scratch_shapes=[
             pltpu.VMEM(x.shape, x.dtype) for x in inputs
@@ -499,11 +501,11 @@
         ]
         + [pltpu.SemaphoreType.DMA] * 5
         + [pltpu.SemaphoreType.DMA((3,))] * 2
-        + [pltpu.SemaphoreType.DMA((12,)), pltpu.SemaphoreType.REGULAR],
+        + [pltpu.SemaphoreType.DMA((11,)), pltpu.SemaphoreType.REGULAR],
         compiler_params=pltpu.CompilerParams(
             collective_id=0, has_side_effects=True, vmem_limit_bytes=63 * 1024 * 1024
         ),
-    )(frames, *inputs)
+    )(counts, start, frames, *inputs)
     spectrum = pl.pallas_call(
         deposit,
         out_shape=jax.ShapeDtypeStruct((6, 2, 4 * AZ), F32),

time: 32.2 us -> 31.7 us (0.984)
  other arithmetic: 0.59 us -> 0 us
    reshape x1 -> x0, other arithmetic: 0.59 us -> none  [on_device(): jnp.concatenate([counts, start]).reshape(1, 2)]
where the time goes in v3:
time: 31.7 us; the launch traced here: 31.5 us
  Pallas kernels  30.2 us (95%)
  between operations  1.3 us (4%)
    pallas_call x1, Pallas kernels, on_device(): pl.pallas_call(correlate_and_send, out_shape=jax.ShapeDtypeStruct((N_TILE...  28.3 us
    pallas_call x1, Pallas kernels, on_device(): pl.pallas_call(deposit, out_shape=jax.ShapeDtypeStruct((6, 2, 4 * AZ), F3...  1.93 us

profile of v3, /device:TPU:1, one launch (start us, length us, event | category | flops | bytes accessed | tf_op | source)
XLA Modules:
  0.0 31.5 jit_solution(16232640955282771162)
XLA Ops:
  1.3 28.3 %shard_map.136.got_ref = f32[32,128]{1,0:T(8,128)} custom-call(s32[1]{0:T(128)S(6)} %copy.15.counts, s32[1]{0:T(128)S(6)} %copy.16.start, bf16[1,4,128,1024]{3,2,1,0:T(8,128)(2,1)} %frames.1, bf16[2,256,256]{2,1,0:T(8,128)(2,1)} %constant.12.clone.refs_0_, bf16[2,256,256]{2,1,0:T(8,128)(2,1)} %constant.13.clone.refs_1_, ...), custom_call_target="tpu_custom_call" | custom-call | tf_op jit(solution)/shard_map/pallas_call | solution.py:482
  29.6 1.9 %shard_map.137 = f32[6,2,2048]{2,1,0:T(2,128)} custom-call(f32[32,128]{1,0:T(8,128)} %shard_map.136.got_ref), custom_call_target="tpu_custom_call" | custom-call | tf_op jit(solution)/shard_map/pallas_call | solution.py:509

commit v4 on v3

--- a/solution.py
+++ b/solution.py
@@ -283,14 +283,19 @@
         pixels = jnp.concatenate(rows, axis=0)
         return dot(pixels, fx[0]) + dot(pixels, fx[1])
 
-    x_hi, x_lo = split2(x_transform([image[f] for f in range(4)]))
-    ts, edges = [], []
+    last, first = tile == N_TILE - 1, tile == 0
+    mean_lane = (iota((1, GROUP), 1) < 128) & (iota((1, GROUP), 1) % HALF == 0)
+    x = x_transform([image[f] for f in range(4)])
+    ts, edges, levels = [], [], []
     for g in range(4):
         t = []
         for f in range(4):
             at = (g * 4 + f) * 128
-            hi, lo = x_hi[at : at + 128], x_lo[at : at + 128]
-            edges.append((hi[96:], lo[96:]) if f < 2 else (hi[:HALF], lo[:HALF]))
+            level = jnp.where(mean_lane, x[at : at + 1], 0.0)
+            hi, lo = split2(x[at : at + 128] - level)
+            levels.append(level)
+            top = jnp.where(first, 0.0, x[at : at + HALF]) - level
+            edges.append((hi[96:], lo[96:]) if f < 2 else split2(top))
             t.append(dot(fy2[...], jnp.concatenate([hi, lo], axis=0)) + dot(fy_lo[...], hi))
         ts.append(t)
     correlate(ts, 3, lambda cam, r: 8 * cam + r, lambda cam, r: r)
@@ -326,24 +331,18 @@
 
     halos[0].wait()
     halos[1].wait()
-    x_hi, x_lo = split2(
-        x_transform([from_below[0], from_below[1], from_above[0], from_above[1]])
-    )
-    last, first = tile == N_TILE - 1, tile == 0
+    x = x_transform([from_below[0], from_below[1], from_above[0], from_above[1]])
+    keep = jnp.where(last, 0.0, 1.0)
     ts = []
     for g in range(4):
         t = []
         for f in range(4):
-            at = (g * 4 + f) * HALF
-            there = [x_hi[at : at + HALF], x_lo[at : at + HALF]]
-            here = edges[g * 4 + f]
-            if f < 2:
-                there = [jnp.where(last, 0.0, x.astype(F32)).astype(BF) for x in there]
-                hi, lo = [[a, b] for a, b in zip(here, there)]
-            else:
-                here = [jnp.where(first, 0.0, x.astype(F32)).astype(BF) for x in here]
-                hi, lo = [[a, b] for a, b in zip(there, here)]
-            t.append(dot(fyb[...], jnp.concatenate(hi + lo + hi, axis=0)))
+            i = g * 4 + f
+            part = x[i * HALF : (i + 1) * HALF]
+            there = split2((part * keep if f < 2 else part) - levels[i])
+            upper, lower = (edges[i], there) if f < 2 else (there, edges[i])
+            (hi0, lo0), (hi1, lo1) = upper, lower
+            t.append(dot(fyb[...], jnp.concatenate([hi0, hi1, lo0, lo1, hi0, hi1], axis=0)))
         ts.append(t)
     correlate(ts, 1, lambda cam, r: 3 + 24 * cam, lambda cam, r: 3 + cam)
 
@@ -374,7 +373,8 @@
     own = six_rows(calib2, list(enumerate(disp)), live[0:1])
     disp = displacement(y_above, peak_above, 1)
     other = six_rows(calib_above, list(enumerate(disp, 2)), jnp.where(across, live_above, 0.0))
-    vecs[pl.ds(tm, 1)] = jnp.concatenate([own, other], axis=0)[None]
+    left = iota((8, 128), 1) < WINS
+    vecs[pl.ds(tm, 1)] = jnp.where(left, own, other)[None]
 
     def vec_copy(i):
         peer = lax.rem(tm + i, N_TM)
@@ -393,8 +393,12 @@
     pltpu.make_async_copy(vecs.at[pl.ds(0, 7)], vecs.at[pl.ds(0, 7)], vec_send).wait()
     pl.semaphore_wait(round_sem, 2)
     pltpu.make_async_copy(vecs.at[pl.ds(0, 7)], vecs.at[pl.ds(0, 7)], vec_recv).wait()
-    def summed(k, rows):
-        return sum(coefs[k * N_TM + s] * vecs[s, rows] for s in range(N_TM))
+    own, other = [], []
+    for k in range(2):
+        total = sum(coefs[k * N_TM + s] * vecs[s] for s in range(N_TM))
+        turned = pltpu.roll(total, WINS, 1)
+        own.append(jnp.where(left, total, turned))
+        other.append(jnp.where(left, turned, total))
 
     first = iota((32, 128), 1) < WINS
     blank = jnp.zeros((WINS, 128), F32)
@@ -408,11 +412,8 @@
         )
         return sum(dot_t(place, piece) for piece in split2(table))
 
-    own, other = slice(0, 8), slice(8, 16)
-    payload = jnp.concatenate([summed(0, own), summed(1, own), spread2, cells], axis=0)
-    payload_above = jnp.concatenate(
-        [summed(0, other), summed(1, other), jnp.zeros((16, 128), F32)], axis=0
-    )
+    payload = jnp.concatenate(own + [spread2, cells], axis=0)
+    payload_above = jnp.concatenate(other + [jnp.zeros((16, 128), F32)], axis=0)
     outbox[:, 0:1] = message(place, payload).reshape(N_TILE, 1, 128)
     outbox[:, 1:2] = message(place_above, payload_above).reshape(N_TILE, 1, 128)
 
@@ -495,7 +496,7 @@
             pltpu.VMEM((24, 128), F32),
             pltpu.VMEM((32, width), F32),
             pltpu.VMEM((40, width), F32),
-            pltpu.VMEM((N_TM, 16, 128), F32),
+            pltpu.VMEM((N_TM, 8, 128), F32),
             pltpu.VMEM((N_TILE, 2, 128), F32),
             pltpu.VMEM((N_TILE, 2, 128), F32),
         ]

time: 31.7 us -> 31.6 us (level)
  no operation moved by 1% of the time
where the time goes in v4:
time: 31.6 us; the launch traced here: 31.5 us
  Pallas kernels  30.2 us (96%)
  between operations  1.3 us (4%)
    pallas_call x1, Pallas kernels, on_device(): pl.pallas_call(correlate_and_send, out_shape=jax.ShapeDtypeStruct((N_TILE...  28.2 us
    pallas_call x1, Pallas kernels, on_device(): pl.pallas_call(deposit, out_shape=jax.ShapeDtypeStruct((6, 2, 4 * AZ), F3...  1.93 us

profile of v4, /device:TPU:1, one launch (start us, length us, event | category | flops | bytes accessed | tf_op | source)
XLA Modules:
  0.0 31.5 jit_solution(12305763566811967347)
XLA Ops:
  1.3 28.2 %shard_map.136.got_ref = f32[32,128]{1,0:T(8,128)} custom-call(s32[1]{0:T(128)S(6)} %copy.15.counts, s32[1]{0:T(128)S(6)} %copy.16.start, bf16[1,4,128,1024]{3,2,1,0:T(8,128)(2,1)} %frames.1, bf16[2,256,256]{2,1,0:T(8,128)(2,1)} %constant.12.clone.refs_0_, bf16[2,256,256]{2,1,0:T(8,128)(2,1)} %constant.13.clone.refs_1_, ...), custom_call_target="tpu_custom_call" | custom-call | tf_op jit(solution)/shard_map/pallas_call | solution.py:483
  29.5 1.9 %shard_map.137 = f32[6,2,2048]{2,1,0:T(2,128)} custom-call(f32[32,128]{1,0:T(8,128)} %shard_map.136.got_ref), custom_call_target="tpu_custom_call" | custom-call | tf_op jit(solution)/shard_map/pallas_call | solution.py:510

commit v5 on v4

--- a/solution.py
+++ b/solution.py
@@ -61,12 +61,13 @@
     fyb_hi, fyb_lo = _pair(fyb)
     iy_hi, iy_lo = _pair(iy)
     cat = np.concatenate
+    halves = slice(0, HALF), slice(HALF, WIN)
     return (
         np.stack([fx_hi, fx_lo]),
         np.stack([ix_hi, ix_lo]),
         cat([fy_hi, fy_hi], axis=1),
         fy_lo,
-        cat([fyb_hi, fyb_hi, fyb_lo], axis=1),
+        np.stack([cat([fyb_hi[:, h], fyb_hi[:, h], fyb_lo[:, h]], axis=1) for h in halves]),
         cat([iy_hi, iy_hi, iy_lo], axis=1),
     )
 
@@ -324,6 +325,11 @@
                 value = jnp.where(n == step, math.cos(2.0 * math.pi * step / 16), value)
             coefs.append(value)
 
+    def half_transform(half, hi, lo):
+        return dot(fyb[half], jnp.concatenate([hi, lo, hi], axis=0))
+
+    here = [half_transform(int(i % 4 >= 2), *edge) for i, edge in enumerate(edges)]
+
     halos[2].wait()
     place_above = places(pack_in[16:17])
     peak_above, calib_above, live_above = pack_in[12:16], pack_in[0:12], pack_in[17:18]
@@ -340,9 +346,7 @@
             i = g * 4 + f
             part = x[i * HALF : (i + 1) * HALF]
             there = split2((part * keep if f < 2 else part) - levels[i])
-            upper, lower = (edges[i], there) if f < 2 else (there, edges[i])
-            (hi0, lo0), (hi1, lo1) = upper, lower
-            t.append(dot(fyb[...], jnp.concatenate([hi0, hi1, lo0, lo1, hi0, hi1], axis=0)))
+            t.append(here[i] + half_transform(int(f < 2), *there))
         ts.append(t)
     correlate(ts, 1, lambda cam, r: 3 + 24 * cam, lambda cam, r: 3 + cam)
 

time: 31.6 us -> 31.7 us (level)
  no operation moved by 1% of the time
where the time goes in v5:
time: 31.7 us; the launch traced here: 31.5 us
  Pallas kernels  30.2 us (95%)
  between operations  1.3 us (4%)
    pallas_call x1, Pallas kernels, on_device(): pl.pallas_call(correlate_and_send, out_shape=jax.ShapeDtypeStruct((N_TILE...  28.3 us
    pallas_call x1, Pallas kernels, on_device(): pl.pallas_call(deposit, out_shape=jax.ShapeDtypeStruct((6, 2, 4 * AZ), F3...  1.93 us

profile of v5, /device:TPU:1, one launch (start us, length us, event | category | flops | bytes accessed | tf_op | source)
XLA Modules:
  0.0 31.5 jit_solution(5729035807639341706)
XLA Ops:
  1.3 28.3 %shard_map.136.got_ref = f32[32,128]{1,0:T(8,128)} custom-call(s32[1]{0:T(128)S(6)} %copy.15.counts, s32[1]{0:T(128)S(6)} %copy.16.start, bf16[1,4,128,1024]{3,2,1,0:T(8,128)(2,1)} %frames.1, bf16[2,256,256]{2,1,0:T(8,128)(2,1)} %constant.12.clone.refs_0_, bf16[2,256,256]{2,1,0:T(8,128)(2,1)} %constant.13.clone.refs_1_, ...), custom_call_target="tpu_custom_call" | custom-call | tf_op jit(solution)/shard_map/pallas_call | solution.py:487
  29.6 1.9 %shard_map.137 = f32[6,2,2048]{2,1,0:T(2,128)} custom-call(f32[32,128]{1,0:T(8,128)} %shard_map.136.got_ref), custom_call_target="tpu_custom_call" | custom-call | tf_op jit(solution)/shard_map/pallas_call | solution.py:514
